TPU v7x, 32 devices: a whole 2x2x4 slice. The times are simulated.
32 devices in a mesh: fsdp: 16 (over z, y, x), tp: 2 (over core).
Axes of the slice: x: 2, y: 2, z: 4, core: 2. Of those that a mesh axis runs over, the one named last changes fastest.
Arguments:
- activations: bfloat16 [256, 18432], P('fsdp', 'tp'), may hold values from -6 to 6
- down_weight: bfloat16 [4608, 18432], P('fsdp', 'tp'), may hold values from -0.046875 to 0.046875
- basis: bfloat16 [8, 4608, 18432], P(None, 'fsdp', 'tp'), may hold values from -64 to 64, as said below
- target: bfloat16 [4608, 256], P('fsdp'), may hold values from -6 to 6
Outputs:
- new_vector: float32 [4608, 18432], P('fsdp', 'tp')
- hessenberg: float32 [9], replicated
Inputs may be any that keep to these rules, and one draw needn't show every extreme that they name: The basis vectors are linearly independent and not orthogonal.
All inputs are finite; a program needn't handle non-finite values.
Results may differ from a plain program's by a relative error of at most 0.00055.
Values may be sent and summed in bfloat16 or wider, within the bound.
A program may use at most 256 MiB of HBM per device.

v0:
```python
import jax
import jax.numpy as jnp
from jax import lax
from jax.sharding import PartitionSpec as P

D = 4608
FFW = 18432


def body(activations, down_weight, basis, target):
    count = float(D * FFW)
    total_tokens = target.shape[1]
    local_rows = down_weight.shape[0]
    basis_count = basis.shape[0]
    basis_flat = basis.reshape(basis_count, -1)
    gram = (
        lax.psum(
            lax.dot_general(
                basis_flat, basis_flat, (((1,), (1,)), ((), ())), preferred_element_type=jnp.float32
            ),
            ("fsdp", "tp"),
        )
        / count
    )
    both = jnp.concatenate([down_weight, basis[basis_count - 1]], 0)
    proj = lax.dot_general(
        both,
        lax.all_gather(activations, "fsdp", axis=0, tiled=True),
        (((1,), (1,)), ((), ())),
        preferred_element_type=jnp.float32,
    )
    summed = lax.psum(proj, "tp")
    slope = jnp.tanh(summed[:local_rows] - target.astype(jnp.float32))
    weighted = ((1.0 - slope * slope) * summed[local_rows:]).astype(jnp.bfloat16)
    hvp = jnp.dot(
        weighted,
        lax.all_gather(activations, "fsdp", axis=0, tiled=True),
        preferred_element_type=jnp.float32,
    ) / float(total_tokens)
    flat = hvp.reshape(1, -1)
    upper = flat.astype(jnp.bfloat16)
    lower = (flat - upper.astype(jnp.float32)).astype(jnp.bfloat16)
    panel = jnp.concatenate([upper, lower], 0)
    pairs = lax.dot_general(
        basis_flat, panel, (((1,), (1,)), ((), ())), preferred_element_type=jnp.float32
    )
    products, total_sq = lax.psum((jnp.sum(pairs, axis=1), jnp.sum(hvp * hvp)), ("fsdp", "tp"))
    products = products / count
    total_sq = total_sq / count
    second = products - jnp.dot(gram, products, precision=lax.Precision.HIGHEST)
    coeffs = products + second
    result = hvp
    for index in range(basis_count):
        result = result - coeffs[index] * basis[index].astype(jnp.float32)
    squares = (
        total_sq
        - 2.0 * jnp.sum(coeffs * products)
        + jnp.sum(coeffs * jnp.dot(gram, coeffs, precision=lax.Precision.HIGHEST))
    )
    beta = jnp.sqrt(squares)
    new_vector = result / beta
    hessenberg = jnp.concatenate([products + second, beta[None]])
    return (new_vector, hessenberg)


def solution(mesh):
    return jax.shard_map(
        body,
        mesh=mesh,
        in_specs=(P("fsdp", "tp"), P("fsdp", "tp"), P(None, "fsdp", "tp"), P("fsdp", None)),
        out_specs=(P("fsdp", "tp"), P()),
        check_vma=False,
    )
```

profile of v0, /device:TPU:0, one launch (start us, length us, event | category | flops | bytes accessed | tf_op | source)
XLA Modules:
  0.0 466.6 jit_solution(18034391575690582681)
XLA Ops:
  7.2 0.0 all-gather.2.cloned.1.call-start
  7.2 0.7 all-gather.2.cloned.1.call-update
  7.9 0.0 all-reduce.3.cloned.1.call-start
  7.9 5.2 %slice_bitcast_fusion = bf16[288,9216]{1,0:T(8,128)(2,1)} fusion(bf16[8,288,9216]{2,1,0:T(8,128)(2,1)} %param.6), kind=kLoop, calls=%fused_computation.22 | loop fusion | bytes 10616832 | tf_op jit(solution)/shard_map/squeeze | solution.py:25
  13.2 80.8 %all-gather.2.cloned.1.call-done = bf16[256,9216]{1,0:T(8,128)(2,1)} async-done(((bf16[16,9216]{1,0:T(8,128)(2,1)}), bf16[256,9216]{1,0:T(8,128)(2,1)}) %all-gather.2.cloned.1.call-update) | async-done | bytes 4718608 | tf_op jit(solution)/shard_map/all_gather | solution.py:28
  94.0 9.2 %fusion.2 = f32[576,256]{1,0:T(8,128)} fusion(bf16[256,9216]{1,0:T(8,128)(2,1)} %all-gather.2.cloned.1.call-done, bf16[288,9216]{1,0:T(8,128)(2,1)} %slice_bitcast_fusion, bf16[288,9216]{1,0:T(8,128)(2,1)} %param.5), kind=kOutput, calls=%fused_computation.3 | convolution fusion | flops 2739142656 | bytes 15925248 | tf_op jit(solution)/shard_map/dot_general | solution.py:26
  103.2 0.0 all-reduce.3.cloned.1.call-update
  103.2 137.7 %fusion.12 = f32[8,8]{1,0:T(8,128)S(1)} fusion(bf16[8,288,9216]{2,1,0:T(8,128)(2,1)} %param.6), kind=kOutput, calls=%fused_computation.23 | convolution fusion | flops 339738624 | bytes 42467584 | tf_op jit(solution)/shard_map/dot_general | solution.py:18
  240.9 0.0 copy-start.1
  241.0 52.6 %copy.9 = bf16[1,8,288,9216]{3,1,2,0:T(8,128)(2,1)} copy(bf16[1,8,288,9216]{3,2,1,0:T(8,128)(2,1)} %bitcast.73) | data formatting | bytes 84934656
  293.5 0.0 all-reduce.3.cloned.1.call-done
  293.6 0.0 copy-done.1
  293.6 6.1 %multiply_reduce_fusion = (f32[]{:T(128)}, f32[288,9216]{1,0:T(8,128)S(1)}) fusion(bf16[256,9216]{1,0:T(8,128)(2,1)} %all-gather.2.cloned.1.call-done, f32[576,256]{1,0:T(8,128)} %all-reduce.3.cloned.1.call-done, bf16[288,256]{1,0:T(8,128)(2,1)S(1)} %copy-done.1), kind=kOutput, calls=%fused_computation.20 | convolution fusion | flops 1367359488 | bytes 16072708 | tf_op jit(solution)/shard_map/dot_general | solution.py:35
  299.6 32.2 %copy.8 = f32[1,1,288,9216]{3,1,2,0:T(1,128)S(1)} copy(f32[1,1,288,9216]{3,2,1,0:T(8,128)S(1)} %bitcast.74) | data formatting | bytes 21233664
  331.8 0.0 copy-done
  331.8 8.9 %convert_element_type.76 = bf16[1,2654208]{1,0:T(2,128)(2,1)} convert(f32[1,2654208]{1,0:T(1,128)S(1)} %bitcast.75) | non-fusion elementwise | flops 2654208 | bytes 15925248 | tf_op jit(solution)/shard_map/convert_element_type | solution.py:41
  340.8 8.7 %subtract_convert_fusion = bf16[1,2654208]{1,0:T(2,128)(2,1)} fusion(f32[1,2654208]{1,0:T(1,128)S(1)} %bitcast.76), kind=kLoop, calls=%fused_computation.21 | loop fusion | flops 10616832 | bytes 15925248 | tf_op jit(solution)/shard_map/convert_element_type | solution.py:42
  349.4 37.5 %fusion.15 = f32[8]{0:T(128)S(1)} fusion(bf16[8,2654208]{1,0:T(8,128)(2,1)} %bitcast.77, bf16[1,2654208]{1,0:T(2,128)(2,1)} %subtract_convert_fusion, bf16[1,2654208]{1,0:T(2,128)(2,1)} %convert_element_type.76), kind=kOutput, calls=%fused_computation.26 | convolution fusion | flops 106168328 | bytes 53084192 | tf_op jit(solution)/shard_map/dot_general | solution.py:44
  387.0 39.8 %all-reduce = (f32[]{:T(128)}, f32[8,8]{1,0:T(8,128)S(1)}, f32[8]{0:T(128)S(1)}) all-reduce(f32[]{:T(128)} %get-tuple-element.13, f32[8,8]{1,0:T(8,128)S(1)} %fusion.12, f32[8]{0:T(128)S(1)} %fusion.15), channel_id=1, replica_groups=mesh['fsdp'=16,'tp'=2] {'fsdp','tp'}, use_global_device_ids=true, to_apply=%region_5.0 | all-reduce | flops 73 | bytes 584 | tf_op jit(solution)/shard_map/psum | solution.py:47
  426.7 0.7 multiply_reduce_fusion.1
  427.5 0.8 fusion.21
  428.3 0.7 fusion.41
  430.9 0.6 pad_maximum_fusion
  431.5 27.9 %fusion.11 = f32[288,9216]{1,0:T(8,128)} fusion(f32[288,9216]{1,0:T(8,128)} %copy-done, f32[]{:T(128)} %sqrt.3, f32[]{:T(128)} %bitcast.18, bf16[8,288,9216]{2,1,0:T(8,128)(2,1)} %param.6, f32[]{:T(128)} %bitcast.16, f32[]{:T(128)} %bitcast.14, f32[]{:T(128)} %bitcast.12, f32[]{:T(128)} %bitcast.10, f32[]{:T(128)} %bitcast.8, f32[]{:T(128)} %bitcast.6, ...), kind=kLoop, calls=%fused_computation.13 | loop fusion | flops 66355200 | bytes 63701028 | tf_op jit(solution)/shard_map/div | solution.py:61
  (1 shorter events, 0.0 us)
Async XLA Ops:
  7.2 86.8 %all-gather.2.cloned.1.call-start = ((), (), s32[]{:S(2)}) async-start(), calls=%async_computation | async-start | bytes 5013504 | tf_op jit(solution)/shard_map/all_gather | solution.py:28
  7.9 285.7 %all-reduce.3.cloned.1.call-start = ((), (), s32[]{:S(2)}) async-start(), calls=%async_computation.1 | async-start | bytes 1179648 | tf_op jit(solution)/shard_map/psum | solution.py:32
  240.9 52.6 %copy-start.1 = (bf16[288,256]{1,0:T(8,128)(2,1)S(1)}, bf16[288,256]{1,0:T(8,128)(2,1)}, u32[]{:S(2)}) copy-start(bf16[288,256]{1,0:T(8,128)(2,1)} %param.7) | copy-start | bytes 442372
  299.6 32.2 %copy-start = (f32[288,9216]{1,0:T(8,128)}, f32[288,9216]{1,0:T(8,128)S(1)}, u32[]{:S(2)}) copy-start(f32[288,9216]{1,0:T(8,128)S(1)} %get-tuple-element.14) | copy-start | bytes 31850500
Sparse Core Ops, SparseCore 0:
  10.8 83.1 all-gather.1
  103.3 17.4 all-reduce.2
where the time goes:
time: 467 us
  matrix products  192 us (41%)
  local copies, waits for them, and re-layouts  90.7 us (19%)
  waiting for transfers between devices  81.5 us (17%)
  other arithmetic  46.1 us (10%)
  blocking collectives  39.8 us (9%)
  between operations  16.5 us (4%)
    dot_general x1, matrix products, body(): lax.dot_general(basis_flat, basis_flat, (((1,), (1,)), ((), ())), preferr...  138 us
    unnamed x6, local copies, waits for them, and re-layouts  84.8 us
    all_gather x1, waiting for transfers between devices, body(): lax.all_gather(activations, 'fsdp', axis=0, tiled=True)  80.8 us
    psum x1, blocking collectives, body(): lax.psum((jnp.sum(pairs, axis=1), jnp.sum(hvp * hvp)), ('fsdp', 'tp'))  39.8 us
    dot_general x1, matrix products, body(): lax.dot_general(basis_flat, panel, (((1,), (1,)), ((), ())), preferred_el...  37.5 us
    div x1, other arithmetic, body(): new_vector = result / beta  27.9 us
  transfers between devices with their start and end apart: 2, of which 1 were waited for; matrix products, arithmetic and copies ran while one was open for 42% of the time, Pallas kernels for 0%

commit v1 on v0

--- a/solution.py
+++ b/solution.py
@@ -1,13 +1,22 @@
+import functools
 import jax
 import jax.numpy as jnp
 from jax import lax
+from jax.experimental import pallas as pl
+from jax.experimental.pallas import tpu as pltpu
 from jax.sharding import PartitionSpec as P
 
 D = 4608
 FFW = 18432
-
-
-def body(activations, down_weight, basis, target):
+MESH = pl.DeviceIdType.MESH
+NT = (((1,), (1,)), ((), ()))
+CHUNK = 1024
+HALF = CHUNK // 2
+GROUP = 32
+LAG = 2
+
+
+def plain_body(activations, down_weight, basis, target):
     count = float(D * FFW)
     total_tokens = target.shape[1]
     local_rows = down_weight.shape[0]
@@ -63,9 +72,312 @@
     return (new_vector, hessenberg)
 
 
+def gather_kernel(
+    steps, act_hbm, w_hbm, basis_hbm, target_ref,
+    act_out, weighted_out, coef_out,
+    stack, held, proj, gram, tokgram, other, cur, got, zslots,
+    own_sem, load_w, load_b, z_send, z_recv, s2, r2, s3, r3, out_sem,
+    ex_send, ex_recv, red_send, red_recv,
+):
+    me = lax.axis_index("fsdp")
+    core = lax.axis_index("tp")
+    mz, my, mx = me // 4, (me // 2) % 2, me % 2
+    xnb = {"fsdp": mz * 4 + my * 2 + (1 - mx)}
+    ynb = {"fsdp": mz * 4 + (1 - my) * 2 + mx}
+    tnb = {"tp": 1 - core}
+    rows = w_hbm.shape[0]
+    kb = basis_hbm.shape[0]
+
+    def znb(shift):
+        return {"fsdp": lax.rem(mz + shift, 4) * 4 + my * 2 + mx}
+
+    def cols(t, start=0, size=CHUNK):
+        return pl.ds(pl.multiple_of(t * CHUNK + start, HALF), size)
+
+    own = pltpu.make_async_copy(act_hbm, held.at[mz, my, mx], own_sem)
+    own.start()
+
+    def copy_w(t):
+        return pltpu.make_async_copy(w_hbm.at[:, cols(t)], stack.at[0, :, cols(t)], load_w.at[t])
+
+    def copy_b(t):
+        return pltpu.make_async_copy(
+            basis_hbm.at[:, :, cols(t)], stack.at[pl.ds(1, kb), :, cols(t)], load_b.at[t]
+        )
+
+    @pl.loop(0, steps)
+    def _(t):
+        copy_w(t).start()
+        copy_b(t).start()
+
+    barrier = pltpu.get_barrier_semaphore()
+    for nb in (znb(1), znb(2), znb(3), xnb, ynb, tnb):
+        pl.semaphore_signal(barrier, inc=1, device_id=nb, device_id_type=MESH)
+    proj[...] = jnp.zeros_like(proj)
+    gram[...] = jnp.zeros_like(gram)
+    tokgram[...] = jnp.zeros_like(tokgram)
+    pl.semaphore_wait(barrier, 6)
+    own.wait()
+
+    def copy_z(t, shift, arriving):
+        z = lax.rem(mz + 4 - shift, 4) if arriving else mz
+        part = held.at[z, my, mx, :, cols(t)]
+        return pltpu.make_async_remote_copy(
+            part, part, z_send.at[t, shift - 1], z_recv.at[t, shift - 1],
+            device_id=znb(shift), device_id_type=MESH,
+        )
+
+    def copy_2(t, way, arriving):
+        if way == 0:
+            part = held.at[:, my, (1 - mx) if arriving else mx, :, cols(t, 0, HALF)]
+        else:
+            part = held.at[:, (1 - my) if arriving else my, mx, :, cols(t, HALF, HALF)]
+        return pltpu.make_async_remote_copy(
+            part, part, s2.at[way, t], r2.at[way, t],
+            device_id=xnb if way == 0 else ynb, device_id_type=MESH,
+        )
+
+    def copy_3(t, way, arriving):
+        if way == 0:
+            part = held.at[:, (1 - my) if arriving else my, :, :, cols(t, 0, HALF)]
+        else:
+            part = held.at[:, :, (1 - mx) if arriving else mx, :, cols(t, HALF, HALF)]
+        return pltpu.make_async_remote_copy(
+            part, part, s3.at[way, t], r3.at[way, t],
+            device_id=ynb if way == 0 else xnb, device_id_type=MESH,
+        )
+
+    def copy_out(t):
+        return pltpu.make_async_copy(
+            held.at[:, :, :, :, cols(t)], act_out.at[:, :, :, :, cols(t)], out_sem.at[t]
+        )
+
+    @pl.loop(0, steps)
+    def _(t):
+        for shift in (1, 2, 3):
+            copy_z(t, shift, False).start()
+
+    @pl.loop(0, steps + 2 * LAG)
+    def _(t):
+        @pl.when(t < steps)
+        def _():
+            for shift in (1, 2, 3):
+                copy_z(t, shift, True).wait_recv()
+            copy_2(t, 0, False).start()
+            copy_2(t, 1, False).start()
+
+        @pl.when((t >= LAG) & (t < steps + LAG))
+        def _():
+            u = t - LAG
+            for way in (0, 1):
+                copy_2(u, way, True).wait_recv()
+                copy_3(u, way, False).start()
+
+        @pl.when(t < steps)
+        def _():
+            copy_w(t).wait()
+            copy_b(t).wait()
+
+            @pl.loop(0, rows // GROUP)
+            def _(g):
+                at = pl.ds(pl.multiple_of(g * GROUP, GROUP), GROUP)
+                part = stack[1:, at, cols(t)].reshape(kb * GROUP, CHUNK)
+                gram[...] += lax.dot_general(part, part, NT, preferred_element_type=jnp.float32)
+
+        @pl.when(t >= 2 * LAG)
+        def _():
+            u = t - 2 * LAG
+            copy_3(u, 0, True).wait_recv()
+            copy_3(u, 1, True).wait_recv()
+            copy_out(u).start()
+            act = held[:, :, :, :, cols(u)].reshape(proj.shape[2], CHUNK)
+            tokgram[...] += lax.dot_general(act, act, NT, preferred_element_type=jnp.float32)
+
+            @pl.loop(0, rows // GROUP)
+            def _(g):
+                at = pl.ds(pl.multiple_of(g * GROUP, GROUP), GROUP)
+                part = stack[:, at, cols(u)].reshape((kb + 1) * GROUP, CHUNK)
+                act = held[:, :, :, :, cols(u)].reshape(proj.shape[2], CHUNK)
+                made = lax.dot_general(part, act, NT, preferred_element_type=jnp.float32)
+                proj[:, at, :] += made.reshape(kb + 1, GROUP, proj.shape[2])
+
+    exchange = [
+        pltpu.make_async_remote_copy(
+            proj.at[k], other.at[i], ex_send.at[i], ex_recv.at[i],
+            device_id=tnb, device_id_type=MESH,
+        )
+        for i, k in enumerate((0, kb))
+    ]
+    for copy in exchange:
+        copy.start()
+
+    lane = lax.broadcasted_iota(jnp.int32, (8, 128), 1)
+    row = lax.broadcasted_iota(jnp.int32, (8, 128), 0)
+    size = kb * GROUP
+    r_at = lax.broadcasted_iota(jnp.int32, (size, size), 0)
+    c_at = lax.broadcasted_iota(jnp.int32, (size, size), 1)
+    kept = jnp.where(r_at % GROUP == c_at % GROUP, gram[...], 0.0)
+    sums = jnp.sum(kept.reshape(kb, GROUP, size), axis=1)
+    block = lax.broadcasted_iota(jnp.int32, (kb, size), 1) // GROUP
+    tile = jnp.zeros((8, 128), jnp.float32)
+    for k in range(kb):
+        one = jnp.sum(jnp.where(block == k, sums, 0.0), axis=1, keepdims=True)
+        tile = jnp.where(lane == k, one, tile)
+
+    for copy in exchange:
+        copy.wait()
+    slope = jnp.tanh(proj[0] + other[0] - target_ref[...].astype(jnp.float32))
+    weighted = ((1.0 - slope * slope) * (proj[kb] + other[1])).astype(jnp.bfloat16)
+    weighted_out[...] = weighted
+    wide = weighted.astype(jnp.float32)
+    for k in range(kb):
+        one = jnp.sum(jnp.sum(wide * proj[k + 1], axis=0, keepdims=True), axis=1, keepdims=True)
+        tile = jnp.where((lane == 8) & (row == k), one, tile)
+    pairs = lax.dot_general(
+        weighted, weighted, (((0,), (0,)), ((), ())), preferred_element_type=jnp.float32
+    )
+    square = jnp.sum(jnp.sum(pairs * tokgram[...], axis=0, keepdims=True), axis=1, keepdims=True)
+    tile = jnp.where((lane == 9) & (row == 0), square, tile)
+
+    for i, nb in enumerate((tnb, xnb, ynb)):
+        cur[i] = tile
+        copy = pltpu.make_async_remote_copy(
+            cur.at[i], got.at[i], red_send.at[i], red_recv.at[i], device_id=nb, device_id_type=MESH
+        )
+        copy.start()
+        copy.wait()
+        tile = tile + got[i]
+    zslots[mz] = tile
+    for shift in (1, 2, 3):
+        pltpu.make_async_remote_copy(
+            zslots.at[mz], zslots.at[mz], red_send.at[2 + shift], red_recv.at[2 + shift],
+            device_id=znb(shift), device_id_type=MESH,
+        ).start()
+    for shift in (1, 2, 3):
+        z = lax.rem(mz + 4 - shift, 4)
+        copy = pltpu.make_async_remote_copy(
+            zslots.at[mz], zslots.at[z], red_send.at[2 + shift], red_recv.at[2 + shift],
+            device_id=znb(shift), device_id_type=MESH,
+        )
+        copy.wait_recv()
+        copy.wait_send()
+    total = (zslots[0] + zslots[1]) + (zslots[2] + zslots[3])
+
+    count = float(D * FFW)
+    tokens = float(target_ref.shape[1])
+
+    def over(x):
+        return jnp.sum(x, axis=1, keepdims=True)
+
+    def down(x):
+        return jnp.sum(x, axis=0, keepdims=True)
+
+    gm = jnp.where(lane < kb, total, 0.0) / count
+    p_col = over(jnp.where(lane == 8, total, 0.0)) / (count * tokens)
+    total_sq = down(over(jnp.where((lane == 9) & (row == 0), total, 0.0))) / (
+        count * tokens * tokens
+    )
+    p_row = down(jnp.where(row == lane, p_col, 0.0))
+    c_row = p_row + (p_row - down(gm * p_col))
+    c_col = over(jnp.where(row == lane, c_row, 0.0))
+    squares = total_sq - 2.0 * over(c_row * p_row) + over(c_row * down(gm * c_col))
+    beta = jnp.sqrt(squares)
+    coef_out[0:8] = jnp.where(lane == 0, c_col / beta, c_col)
+    coef_out[8:16] = jnp.where(row == 0, 1.0 / (beta * tokens), beta)
+
+    @pl.loop(0, steps)
+    def _(t):
+        copy_out(t).wait()
+        for shift in (1, 2, 3):
+            copy_z(t, shift, False).wait_send()
+        for way in (0, 1):
+            copy_2(t, way, False).wait_send()
+            copy_3(t, way, False).wait_send()
+
+
+def finish_kernel(coef, weighted, act, basis, out, hess, field):
+    kb = basis.shape[0]
+    field[...] = jnp.dot(weighted[...], act[...], preferred_element_type=jnp.float32)
+    scale = coef[8, 0]
+
+    @pl.loop(0, out.shape[0] // 16)
+    def _(g):
+        at = pl.ds(pl.multiple_of(g * 16, 16), 16)
+        acc = field[at, :] * scale
+        for k in range(kb):
+            acc = acc - coef[k, 0] * basis[k, at, :].astype(jnp.float32)
+        out[at, :] = acc
+
+    for k in range(kb):
+        hess[k] = coef[k, 1]
+    hess[kb] = coef[9, 0]
+
+
+def kernel_body(activations, down_weight, basis, target):
+    kb, rows, hidden = basis.shape
+    own_tokens = activations.shape[0]
+    tokens = target.shape[1]
+    steps = hidden // CHUNK
+    f32, bf16 = jnp.float32, jnp.bfloat16
+    any_spec = pl.BlockSpec(memory_space=pl.ANY)
+    vmem = pl.BlockSpec(memory_space=pltpu.VMEM)
+    dma = pltpu.SemaphoreType.DMA
+    act, weighted, coef = pl.pallas_call(
+        functools.partial(gather_kernel, steps),
+        out_shape=(
+            jax.ShapeDtypeStruct((4, 2, 2, own_tokens, hidden), bf16),
+            jax.ShapeDtypeStruct((rows, tokens), bf16),
+            jax.ShapeDtypeStruct((16, 128), f32),
+        ),
+        in_specs=[any_spec, any_spec, any_spec, vmem],
+        out_specs=(any_spec, vmem, vmem),
+        scratch_shapes=[
+            pltpu.VMEM((kb + 1, rows, hidden), bf16),
+            pltpu.VMEM((4, 2, 2, own_tokens, hidden), bf16),
+            pltpu.VMEM((kb + 1, rows, tokens), f32),
+            pltpu.VMEM((kb * GROUP, kb * GROUP), f32),
+            pltpu.VMEM((tokens, tokens), f32),
+            pltpu.VMEM((2, rows, tokens), f32),
+            pltpu.VMEM((3, 8, 128), f32),
+            pltpu.VMEM((3, 8, 128), f32),
+            pltpu.VMEM((4, 8, 128), f32),
+            dma, dma((steps,)), dma((steps,)),
+            dma((steps, 3)), dma((steps, 3)),
+            dma((2, steps)), dma((2, steps)), dma((2, steps)), dma((2, steps)),
+            dma((steps,)),
+            dma((2,)), dma((2,)), dma((6,)), dma((6,)),
+        ],
+        compiler_params=pltpu.CompilerParams(
+            collective_id=0, has_side_effects=True, vmem_limit_bytes=62 * 1024 * 1024
+        ),
+    )(activations, down_weight, basis, target)
+    act = act.reshape(tokens, hidden)
+    return pl.pallas_call(
+        finish_kernel,
+        grid=(steps,),
+        out_shape=(
+            jax.ShapeDtypeStruct((rows, hidden), f32),
+            jax.ShapeDtypeStruct((kb + 1,), f32),
+        ),
+        in_specs=[
+            pl.BlockSpec(memory_space=pltpu.SMEM),
+            pl.BlockSpec((rows, tokens), lambda i: (0, 0)),
+            pl.BlockSpec((tokens, CHUNK), lambda i: (0, i)),
+            pl.BlockSpec((kb, rows, CHUNK), lambda i: (0, 0, i)),
+        ],
+        out_specs=(
+            pl.BlockSpec((rows, CHUNK), lambda i: (0, i)),
+            pl.BlockSpec(memory_space=pltpu.SMEM),
+        ),
+        scratch_shapes=[pltpu.VMEM((rows, CHUNK), f32)],
+        compiler_params=pltpu.CompilerParams(vmem_limit_bytes=48 * 1024 * 1024),
+    )(coef, weighted, act, basis)
+
+
 def solution(mesh):
+    fits = mesh.shape["fsdp"] == 16 and mesh.shape["tp"] == 2
     return jax.shard_map(
-        body,
+        kernel_body if fits else plain_body,
         mesh=mesh,
         in_specs=(P("fsdp", "tp"), P("fsdp", "tp"), P(None, "fsdp", "tp"), P("fsdp", None)),
         out_specs=(P("fsdp", "tp"), P()),

time: 467 us -> 119 us (0.25)
  matrix products: 192 us -> 0 us
  Pallas kernels: 0 us -> 114 us
  local copies, waits for them, and re-layouts: 90.7 us -> 3.94 us
  waiting for transfers between devices: 81.5 us -> 0 us
  other arithmetic: 46.1 us -> 0 us
  blocking collectives: 39.8 us -> 0 us
  between operations: 16.5 us -> 0.65 us
    dot_general x6 -> x0, matrix products: 192 us -> none  [the longest x1 138 us: body(): lax.dot_general(basis_flat, basis_flat, (((1,), (1,)), ((), ())), preferr...]
    pallas_call x0 -> x2, Pallas kernels: none -> 114 us  [the longest x1 90.9 us: kernel_body(): pl.pallas_call(functools.partial(gather_kernel, steps), out_shape=(jax.Sh...]
    unnamed x6, local copies, waits for them, and re-layouts: 84.8 us -> 3.94 us
    all_gather x1 -> x0, waiting for transfers between devices: 80.8 us -> none  [body(): lax.all_gather(activations, 'fsdp', axis=0, tiled=True)]
    psum x1 -> x0, blocking collectives: 39.8 us -> none  [body(): lax.psum((jnp.sum(pairs, axis=1), jnp.sum(hvp * hvp)), ('fsdp', 'tp'))]
    div x1 -> x0, other arithmetic: 27.9 us -> none  [body(): new_vector = result / beta]
    convert_element_type x2 -> x0, other arithmetic: 17.6 us -> none  [the longest x1 8.93 us: body(): upper = flat.astype(jnp.bfloat16)]
    squeeze x1 -> x0, local copies, waits for them, and re-layouts: 5.23 us -> none  [body(): both = jnp.concatenate([down_weight, basis[basis_count - 1]], 0)]
  transfers between devices with their start and end apart: 2 -> 0, of which waited for: 1 -> 0; matrix products, arithmetic and copies ran while one was open for 42% -> 0% of each run, Pallas kernels for 0% -> 0%
where the time goes in v1:
time: 119 us
  Pallas kernels  114 us (96%)
  local copies, waits for them, and re-layouts  3.94 us (3%)
    pallas_call x1, Pallas kernels, kernel_body(): pl.pallas_call(functools.partial(gather_kernel, steps), out_shape=(jax.Sh...  90.9 us
    pallas_call x1, Pallas kernels, kernel_body(): pl.pallas_call(finish_kernel, grid=(steps,), out_shape=(jax.ShapeDtypeStr...  23.6 us
    unnamed x6, local copies, waits for them, and re-layouts  3.94 us

profile of v1, /device:TPU:0, one launch (start us, length us, event | category | flops | bytes accessed | tf_op | source)
XLA Modules:
  0.0 119.0 jit_solution(6050067286148550785)
XLA Ops:
  0.6 90.9 %shard_map.59 = (bf16[4,2,2,16,9216]{4,3,2,1,0:T(8,128)(2,1)}, bf16[288,256]{1,0:T(8,128)(2,1)}, f32[16,128]{1,0:T(8,128)}) custom-call(bf16[16,9216]{1,0:T(8,128)(2,1)} %act_hbm.1, bf16[288,9216]{1,0:T(8,128)(2,1)} %w_hbm.1, bf16[8,288,9216]{2,1,0:T(8,128)(2,1)} %basis.1, bf16[288,256]{1,0:T(8,128)(2,1)} %target_ref.1), custom_call_target="tpu_custom_call" | custom-call | tf_op jit(solution)/shard_map/pallas_call | solution.py:325
  91.5 0.0 copy-start
  91.5 2.3 %copy-done = bf16[4,2,2,16,9216]{4,3,2,1,0:T(8,128)(2,1)S(1)} copy-done((bf16[4,2,2,16,9216]{4,3,2,1,0:T(8,128)(2,1)S(1)}, bf16[4,2,2,16,9216]{4,3,2,1,0:T(8,128)(2,1)}, u32[]{:S(2)}) %copy-start) | copy-done | bytes 4718616
  93.8 0.0 copy-start.1
  93.8 0.9 copy-done.1
  94.8 0.0 copy-start.2
  94.8 0.7 copy-done.2
  95.5 23.6 %shard_map.60 = (f32[288,9216]{1,0:T(8,128)}, f32[9]{0:T(128)}) custom-call(f32[16,128]{1,0:T(8,128)S(1)} %copy-done.2, bf16[288,256]{1,0:T(8,128)(2,1)S(1)} %copy-done.1, bf16[256,9216]{1,0:T(8,128)(2,1)S(1)} %bitcast.1, bf16[8,288,9216]{2,1,0:T(8,128)(2,1)} %basis.1), custom_call_target="tpu_custom_call" | custom-call | tf_op jit(solution)/shard_map/pallas_call | solution.py:355
Async XLA Ops:
  91.5 2.3 %copy-start = (bf16[4,2,2,16,9216]{4,3,2,1,0:T(8,128)(2,1)S(1)}, bf16[4,2,2,16,9216]{4,3,2,1,0:T(8,128)(2,1)}, u32[]{:S(2)}) copy-start(bf16[4,2,2,16,9216]{4,3,2,1,0:T(8,128)(2,1)} %get-tuple-element.7) | copy-start | bytes 14155780
  93.8 0.9 copy-start.1
  94.8 0.7 copy-start.2

commit v2 on v1

--- a/solution.py
+++ b/solution.py
@@ -75,9 +75,9 @@
 def gather_kernel(
     steps, act_hbm, w_hbm, basis_hbm, target_ref,
     act_out, weighted_out, coef_out,
-    stack, held, proj, gram, tokgram, other, cur, got, zslots,
+    stack, held, proj, gram, tokgram, other, cube, zslots,
     own_sem, load_w, load_b, z_send, z_recv, s2, r2, s3, r3, out_sem,
-    ex_send, ex_recv, red_send, red_recv,
+    ex_send, ex_recv, cube_send, cube_recv, red_send, red_recv,
 ):
     me = lax.axis_index("fsdp")
     core = lax.axis_index("tp")
@@ -88,6 +88,19 @@
     rows = w_hbm.shape[0]
     kb = basis_hbm.shape[0]
 
+    def cnb(d):
+        y, x = (1 - my) if d & 4 else my, (1 - mx) if d & 2 else mx
+        c = (1 - core) if d & 1 else core
+        return (mz * 4 + y * 2 + x, c), y * 4 + x * 2 + c
+
+    def copy_cube(d, arriving):
+        device, theirs = cnb(d)
+        slot = cube.at[theirs if arriving else my * 4 + mx * 2 + core]
+        return pltpu.make_async_remote_copy(
+            slot, slot, cube_send.at[d - 1], cube_recv.at[d - 1],
+            device_id=device, device_id_type=MESH,
+        )
+
     def znb(shift):
         return {"fsdp": lax.rem(mz + shift, 4) * 4 + my * 2 + mx}
 
@@ -111,12 +124,12 @@
         copy_b(t).start()
 
     barrier = pltpu.get_barrier_semaphore()
-    for nb in (znb(1), znb(2), znb(3), xnb, ynb, tnb):
+    for nb in [znb(1), znb(2), znb(3)] + [cnb(d)[0] for d in range(1, 8)]:
         pl.semaphore_signal(barrier, inc=1, device_id=nb, device_id_type=MESH)
     proj[...] = jnp.zeros_like(proj)
     gram[...] = jnp.zeros_like(gram)
     tokgram[...] = jnp.zeros_like(tokgram)
-    pl.semaphore_wait(barrier, 6)
+    pl.semaphore_wait(barrier, 10)
     own.wait()
 
     def copy_z(t, shift, arriving):
@@ -193,13 +206,9 @@
             act = held[:, :, :, :, cols(u)].reshape(proj.shape[2], CHUNK)
             tokgram[...] += lax.dot_general(act, act, NT, preferred_element_type=jnp.float32)
 
-            @pl.loop(0, rows // GROUP)
-            def _(g):
-                at = pl.ds(pl.multiple_of(g * GROUP, GROUP), GROUP)
-                part = stack[:, at, cols(u)].reshape((kb + 1) * GROUP, CHUNK)
-                act = held[:, :, :, :, cols(u)].reshape(proj.shape[2], CHUNK)
-                made = lax.dot_general(part, act, NT, preferred_element_type=jnp.float32)
-                proj[:, at, :] += made.reshape(kb + 1, GROUP, proj.shape[2])
+            part = stack[:, :, cols(u)].reshape((kb + 1) * rows, CHUNK)
+            made = lax.dot_general(part, act, NT, preferred_element_type=jnp.float32)
+            proj[...] += made.reshape(kb + 1, rows, proj.shape[2])
 
     exchange = [
         pltpu.make_async_remote_copy(
@@ -239,24 +248,24 @@
     square = jnp.sum(jnp.sum(pairs * tokgram[...], axis=0, keepdims=True), axis=1, keepdims=True)
     tile = jnp.where((lane == 9) & (row == 0), square, tile)
 
-    for i, nb in enumerate((tnb, xnb, ynb)):
-        cur[i] = tile
-        copy = pltpu.make_async_remote_copy(
-            cur.at[i], got.at[i], red_send.at[i], red_recv.at[i], device_id=nb, device_id_type=MESH
-        )
-        copy.start()
-        copy.wait()
-        tile = tile + got[i]
+    mine = my * 4 + mx * 2 + core
+    cube[mine] = tile
+    for d in range(1, 8):
+        copy_cube(d, False).start()
+    for d in range(1, 8):
+        copy_cube(d, True).wait_recv()
+        copy_cube(d, False).wait_send()
+    tile = jnp.sum(cube[...], axis=0)
     zslots[mz] = tile
     for shift in (1, 2, 3):
         pltpu.make_async_remote_copy(
-            zslots.at[mz], zslots.at[mz], red_send.at[2 + shift], red_recv.at[2 + shift],
+            zslots.at[mz], zslots.at[mz], red_send.at[shift - 1], red_recv.at[shift - 1],
             device_id=znb(shift), device_id_type=MESH,
         ).start()
     for shift in (1, 2, 3):
         z = lax.rem(mz + 4 - shift, 4)
         copy = pltpu.make_async_remote_copy(
-            zslots.at[mz], zslots.at[z], red_send.at[2 + shift], red_recv.at[2 + shift],
+            zslots.at[mz], zslots.at[z], red_send.at[shift - 1], red_recv.at[shift - 1],
             device_id=znb(shift), device_id_type=MESH,
         )
         copy.wait_recv()
@@ -338,14 +347,13 @@
             pltpu.VMEM((kb * GROUP, kb * GROUP), f32),
             pltpu.VMEM((tokens, tokens), f32),
             pltpu.VMEM((2, rows, tokens), f32),
-            pltpu.VMEM((3, 8, 128), f32),
-            pltpu.VMEM((3, 8, 128), f32),
+            pltpu.VMEM((8, 8, 128), f32),
             pltpu.VMEM((4, 8, 128), f32),
             dma, dma((steps,)), dma((steps,)),
             dma((steps, 3)), dma((steps, 3)),
             dma((2, steps)), dma((2, steps)), dma((2, steps)), dma((2, steps)),
             dma((steps,)),
-            dma((2,)), dma((2,)), dma((6,)), dma((6,)),
+            dma((2,)), dma((2,)), dma((7,)), dma((7,)), dma((3,)), dma((3,)),
         ],
         compiler_params=pltpu.CompilerParams(
             collective_id=0, has_side_effects=True, vmem_limit_bytes=62 * 1024 * 1024
@@ -370,7 +378,7 @@
             pl.BlockSpec(memory_space=pltpu.SMEM),
         ),
         scratch_shapes=[pltpu.VMEM((rows, CHUNK), f32)],
-        compiler_params=pltpu.CompilerParams(vmem_limit_bytes=48 * 1024 * 1024),
+        compiler_params=pltpu.CompilerParams(vmem_limit_bytes=62 * 1024 * 1024),
     )(coef, weighted, act, basis)
 
 

time: 119 us -> 97 us (0.82)
  Pallas kernels: 114 us -> 96.2 us
  local copies, waits for them, and re-layouts: 3.94 us -> 0 us
    pallas_call x1, Pallas kernels: 90.9 us -> 71.7 us  [kernel_body(): pl.pallas_call(functools.partial(gather_kernel, steps), out_shape=(jax.Sh...]
    unnamed x6 -> x0, local copies, waits for them, and re-layouts: 3.94 us -> none
where the time goes in v2:
time: 97 us; the launch traced here: 96.9 us
  Pallas kernels  96.2 us (99%)
    pallas_call x1, Pallas kernels, kernel_body(): pl.pallas_call(functools.partial(gather_kernel, steps), out_shape=(jax.Sh...  71.7 us
    pallas_call x1, Pallas kernels, kernel_body(): pl.pallas_call(finish_kernel, grid=(steps,), out_shape=(jax.ShapeDtypeStr...  24.5 us

profile of v2, /device:TPU:0, one launch (start us, length us, event | category | flops | bytes accessed | tf_op | source)
XLA Modules:
  0.0 96.9 jit_solution(3520378961292222697)
XLA Ops:
  0.6 71.7 %shard_map.59 = (bf16[4,2,2,16,9216]{4,3,2,1,0:T(8,128)(2,1)}, bf16[288,256]{1,0:T(8,128)(2,1)}, f32[16,128]{1,0:T(8,128)}) custom-call(bf16[16,9216]{1,0:T(8,128)(2,1)} %act_hbm.1, bf16[288,9216]{1,0:T(8,128)(2,1)} %w_hbm.1, bf16[8,288,9216]{2,1,0:T(8,128)(2,1)} %basis.1, bf16[288,256]{1,0:T(8,128)(2,1)} %target_ref.1), custom_call_target="tpu_custom_call" | custom-call | tf_op jit(solution)/shard_map/pallas_call | solution.py:334
  72.4 24.5 %shard_map.60 = (f32[288,9216]{1,0:T(8,128)}, f32[9]{0:T(128)}) custom-call(f32[16,128]{1,0:T(8,128)} %get-tuple-element.5.coef, bf16[288,256]{1,0:T(8,128)(2,1)} %get-tuple-element.6.weighted, bf16[256,9216]{1,0:T(8,128)(2,1)} %bitcast.1, bf16[8,288,9216]{2,1,0:T(8,128)(2,1)} %basis.1), custom_call_target="tpu_custom_call" | custom-call | tf_op jit(solution)/shard_map/pallas_call | solution.py:363

commit v3 on v2

--- a/solution.py
+++ b/solution.py
@@ -13,6 +13,7 @@
 CHUNK = 1024
 HALF = CHUNK // 2
 GROUP = 32
+WIDE = 2304
 LAG = 2
 
 
@@ -309,9 +310,9 @@
     field[...] = jnp.dot(weighted[...], act[...], preferred_element_type=jnp.float32)
     scale = coef[8, 0]
 
-    @pl.loop(0, out.shape[0] // 16)
+    @pl.loop(0, out.shape[0] // 32)
     def _(g):
-        at = pl.ds(pl.multiple_of(g * 16, 16), 16)
+        at = pl.ds(pl.multiple_of(g * 32, 32), 32)
         acc = field[at, :] * scale
         for k in range(kb):
             acc = acc - coef[k, 0] * basis[k, at, :].astype(jnp.float32)
@@ -362,7 +363,7 @@
     act = act.reshape(tokens, hidden)
     return pl.pallas_call(
         finish_kernel,
-        grid=(steps,),
+        grid=(hidden // WIDE,),
         out_shape=(
             jax.ShapeDtypeStruct((rows, hidden), f32),
             jax.ShapeDtypeStruct((kb + 1,), f32),
@@ -370,14 +371,14 @@
         in_specs=[
             pl.BlockSpec(memory_space=pltpu.SMEM),
             pl.BlockSpec((rows, tokens), lambda i: (0, 0)),
-            pl.BlockSpec((tokens, CHUNK), lambda i: (0, i)),
-            pl.BlockSpec((kb, rows, CHUNK), lambda i: (0, 0, i)),
+            pl.BlockSpec((tokens, WIDE), lambda i: (0, i)),
+            pl.BlockSpec((kb, rows, WIDE), lambda i: (0, 0, i)),
         ],
         out_specs=(
-            pl.BlockSpec((rows, CHUNK), lambda i: (0, i)),
+            pl.BlockSpec((rows, WIDE), lambda i: (0, i)),
             pl.BlockSpec(memory_space=pltpu.SMEM),
         ),
-        scratch_shapes=[pltpu.VMEM((rows, CHUNK), f32)],
+        scratch_shapes=[pltpu.VMEM((rows, WIDE), f32)],
         compiler_params=pltpu.CompilerParams(vmem_limit_bytes=62 * 1024 * 1024),
     )(coef, weighted, act, basis)
 

time: 97 us -> 93.9 us (0.968)
  Pallas kernels: 96.2 us -> 93.1 us
    pallas_call x1, Pallas kernels: 24.5 us -> 21.4 us  [kernel_body(): pl.pallas_call(finish_kernel, grid=(hidden // WIDE,), out_shape=(jax.Shap...]
where the time goes in v3:
time: 93.9 us; the launch traced here: 93.7 us
  Pallas kernels  93.1 us (99%)
    pallas_call x1, Pallas kernels, kernel_body(): pl.pallas_call(functools.partial(gather_kernel, steps), out_shape=(jax.Sh...  71.7 us
    pallas_call x1, Pallas kernels, kernel_body(): pl.pallas_call(finish_kernel, grid=(hidden // WIDE,), out_shape=(jax.Shap...  21.4 us

profile of v3, /device:TPU:0, one launch (start us, length us, event | category | flops | bytes accessed | tf_op | source)
XLA Modules:
  0.0 93.7 jit_solution(13755904206182644123)
XLA Ops:
  0.6 71.7 %shard_map.59 = (bf16[4,2,2,16,9216]{4,3,2,1,0:T(8,128)(2,1)}, bf16[288,256]{1,0:T(8,128)(2,1)}, f32[16,128]{1,0:T(8,128)}) custom-call(bf16[16,9216]{1,0:T(8,128)(2,1)} %act_hbm.1, bf16[288,9216]{1,0:T(8,128)(2,1)} %w_hbm.1, bf16[8,288,9216]{2,1,0:T(8,128)(2,1)} %basis.1, bf16[288,256]{1,0:T(8,128)(2,1)} %target_ref.1), custom_call_target="tpu_custom_call" | custom-call | tf_op jit(solution)/shard_map/pallas_call | solution.py:335
  72.4 21.4 %shard_map.60 = (f32[288,9216]{1,0:T(8,128)}, f32[9]{0:T(128)}) custom-call(f32[16,128]{1,0:T(8,128)} %get-tuple-element.5.coef, bf16[288,256]{1,0:T(8,128)(2,1)} %get-tuple-element.6.weighted, bf16[256,9216]{1,0:T(8,128)(2,1)} %bitcast.1, bf16[8,288,9216]{2,1,0:T(8,128)(2,1)} %basis.1), custom_call_target="tpu_custom_call" | custom-call | tf_op jit(solution)/shard_map/pallas_call | solution.py:364
